TPU v7x, 128 devices: a whole 4x4x4 slice. The times are simulated.
128 devices in a mesh: ctx: 16 (over z, y), head: 8 (over x, core).
Axes of the slice: x: 4, y: 4, z: 4, core: 2. Of those that a mesh axis runs over, the one named last changes fastest.
Arguments:
- features: bfloat16 [16384, 16384], P('ctx', 'head'), may hold values from -6 to 6
- gates: bfloat16 [16384, 16384], P('ctx', 'head'), may hold values from -6 to 6
- state_io: bfloat16 [16384, 2, 2048], P('ctx', None, 'head'), may hold values from -6 to 6
- step_size: float32 [256, 16384], P('head', 'ctx'), may hold values from 0.004 to 0.02
- log_decay: float32 [256, 16384], P('head', 'ctx'), may hold values from -2 to 0, as said below
- conv_feat: bfloat16 [4, 16384], P(None, 'head'), may hold values from -3 to 3
- conv_state: bfloat16 [4, 2, 2048], P(None, None, 'head'), may hold values from -3 to 3
- skip_gain: float32 [256], P('head'), may hold values from 0.5 to 1.5
- norm_gain: float32 [16384], P('head'), may hold values from 0.25 to 1.75
Outputs:
- mixed: bfloat16 [16384, 16384], P(('ctx', 'head'))
Inputs may be any that keep to these rules, and one draw needn't show every extreme that they name: `log_decay`: every entry is negative.
All inputs are finite; a program needn't handle non-finite values.
Results may differ from a plain program's by a relative error of at most 0.0034.
Values may be sent and summed in bfloat16 or wider, within the bound.
A program may use at most 256 MiB of HBM per device.

v0:
```python
import jax
import jax.numpy as jnp
from jax import lax
from jax.sharding import PartitionSpec as P

STATE = 256
SPAN = 128


def passed_along(value, axis, steps):
    count = lax.axis_size(axis)
    initial, last = (max(0, -steps), min(count, count - steps))
    return lax.ppermute(value, axis, [(source, source + steps) for source in range(initial, last)])


def conv_rows(padded, kernel, length):
    taps = kernel.shape[0]
    summed = jnp.zeros((length,) + padded.shape[1:], jnp.float32)
    for offset in range(taps):
        summed = summed + kernel[offset].astype(jnp.float32) * padded[
            offset : offset + length
        ].astype(jnp.float32)
    return jax.nn.silu(summed).astype(jnp.bfloat16)


def shards(
    features, gates, state_io, step_size, log_decay, conv_feat, conv_state, skip_gain, norm_gain
):
    tok_rows = features.shape[0]
    inner_cols = features.shape[1]
    head_count = step_size.shape[0]
    head_dim = inner_cols // head_count
    state_cols = state_io.shape[2]
    group_count = state_cols // STATE
    per_group = head_count // group_count
    rim_rows = conv_feat.shape[0] - 1
    span_count = tok_rows // SPAN
    tail_rows = jnp.concatenate(
        [
            features[tok_rows - rim_rows :],
            state_io[tok_rows - rim_rows :].reshape(rim_rows, 2 * state_cols),
        ],
        axis=1,
    )
    before = passed_along(tail_rows, "ctx", 1)
    conv_out = conv_rows(
        jnp.concatenate([before[:, :inner_cols], features], axis=0), conv_feat, tok_rows
    )
    conv_io = conv_rows(
        jnp.concatenate(
            [before[:, inner_cols:].reshape(rim_rows, 2, state_cols), state_io], axis=0
        ),
        conv_state,
        tok_rows,
    )
    feat_spans = conv_out.reshape(span_count, SPAN, group_count, per_group, head_dim)
    io_spans = conv_io.reshape(span_count, SPAN, 2, group_count, STATE)
    in_maps = io_spans[:, :, 0]
    out_maps = io_spans[:, :, 1]
    step_spans = step_size.reshape(group_count, per_group, span_count, SPAN).transpose(2, 0, 1, 3)
    cumulated = jnp.cumsum(
        log_decay.reshape(group_count, per_group, span_count, SPAN).transpose(2, 0, 1, 3), axis=3
    )
    scores = jnp.einsum("ctgn,csgn->cgts", out_maps, in_maps, preferred_element_type=jnp.float32)
    lower_mask = jnp.tril(jnp.ones((SPAN, SPAN), dtype=bool))
    gaps = cumulated[..., :, None] - cumulated[..., None, :]
    weights = (
        scores[:, :, None]
        * jnp.exp(jnp.where(lower_mask, gaps, -jnp.inf))
        * step_spans[..., None, :]
    ).astype(jnp.bfloat16)
    output_diag = jnp.einsum(
        "cgjts,csgjp->ctgjp", weights, feat_spans, preferred_element_type=jnp.float32
    )
    span_end = cumulated[..., -1:]
    weighting = jnp.exp(span_end - cumulated) * step_spans
    scaled_in = (
        weighting.transpose(0, 3, 1, 2)[..., None] * feat_spans.astype(jnp.float32)
    ).astype(jnp.bfloat16)
    local_state = jnp.einsum(
        "csgjp,csgn->cgjpn", scaled_in, in_maps, preferred_element_type=jnp.float32
    )
    span_log = span_end[..., 0]

    def advance(carried, pieces):
        log_total, added = pieces
        return (jnp.exp(log_total)[..., None, None] * carried + added, carried)

    zero_state = jnp.zeros(local_state.shape[1:], jnp.float32)
    dev_state, starts = lax.scan(advance, zero_state, (span_log, local_state))
    dev_decay = jnp.exp(jnp.sum(span_log, axis=0))
    start_log = jnp.cumsum(span_log, axis=0) - span_log
    all_decay, all_state = (
        lax.all_gather(dev_decay[None], "ctx", axis=0, tiled=True),
        lax.all_gather(dev_state[None], "ctx", axis=0, tiled=True),
    )
    my_rank = lax.axis_index("ctx")

    def absorb(carried, pieces):
        source_rank, decay_one, state_one = pieces
        return (
            jnp.where(
                source_rank < my_rank, decay_one[..., None, None] * carried + state_one, carried
            ),
            None,
        )

    ranks = jnp.arange(all_decay.shape[0], dtype=jnp.int32)
    incoming, _ = lax.scan(absorb, jnp.zeros_like(dev_state), (ranks, all_decay, all_state))
    span_state = jnp.exp(start_log)[..., None, None] * incoming[None] + starts
    state_low = span_state.astype(jnp.bfloat16)
    output_carried = (
        jnp.einsum("ctgn,cgjpn->ctgjp", out_maps, state_low, preferred_element_type=jnp.float32)
        * jnp.exp(cumulated).transpose(0, 3, 1, 2)[..., None]
    )
    skip_rows = skip_gain.reshape(group_count, per_group)[None, None, :, :, None]
    mixed_in = output_diag + output_carried + skip_rows * feat_spans.astype(jnp.float32)
    gated_out = mixed_in * jax.nn.silu(
        gates.reshape(span_count, SPAN, group_count, per_group, head_dim).astype(jnp.float32)
    )
    mean_square = jnp.mean(gated_out * gated_out, axis=(3, 4), keepdims=True)
    normed = (
        gated_out
        * lax.rsqrt(mean_square + 1e-05)
        * norm_gain.reshape(group_count, per_group, head_dim)
    ).astype(jnp.bfloat16)
    normed = normed.reshape(tok_rows, inner_cols)
    return lax.all_to_all(normed, "head", split_axis=0, concat_axis=1, tiled=True)


def solution(mesh):
    in_specs = (
        P("ctx", "head"),
        P("ctx", "head"),
        P("ctx", None, "head"),
        P("head", "ctx"),
        P("head", "ctx"),
        P(None, "head"),
        P(None, None, "head"),
        P("head"),
        P("head"),
    )
    out_specs = P(("ctx", "head"), None)
    return jax.shard_map(shards, mesh=mesh, in_specs=in_specs, out_specs=out_specs, check_vma=False)
```

profile of v0, /device:TPU:1, one launch (start us, length us, event | category | flops | bytes accessed | tf_op | source)
XLA Modules:
  0.0 438.9 jit_solution(15608546685580111384)
XLA Ops:
  8.0 4.0 collective-permute-start
  13.9 2.3 reduce_window_sum.24
  20.6 13.6 %multiply_convert_fusion.4 = bf16[1024,2048]{1,0:T(8,128)(2,1)} fusion(bf16[1024,2048]{1,0:T(8,128)(2,1)} %param.13, bf16[3,2048]{1,0:T(4,128)(2,1)S(1)} %slice.84, f32[2048]{0:T(1024)S(1)} %bitcast.152, f32[2048]{0:T(1024)S(1)} %bitcast.153, f32[2048]{0:T(1024)S(1)} %bitcast.151, f32[2048]{0:T(1024)S(1)} %bitcast.150), kind=kLoop, calls=%fused_computation.28 | loop fusion | flops 52428800 | bytes 8433664 | tf_op jit(solution)/shard_map/convert_element_type | solution.py:23
  34.3 6.5 %copy.32 = bf16[1024,2048]{0,1:T(8,128)(2,1)} copy(bf16[1024,2048]{1,0:T(8,128)(2,1)} %multiply_convert_fusion.4) | data formatting | bytes 8388608 | tf_op jit(solution)/shard_map/convert_element_type | solution.py:23
  40.7 5.3 %copy.56 = bf16[256,8,8,128]{3,2,1,0:T(8,128)(2,1)} copy(bf16[256,8,8,128]{3,1,2,0:T(8,128)(2,1)} %bitcast.134) | data formatting | bytes 8388608
  46.8 6.0 %fusion.22 = bf16[1024,2,256]{2,1,0:T(2,128)(2,1)S(1)} fusion(bf16[1024,2,256]{2,1,0:T(2,128)(2,1)S(1)} %copy-done.2, bf16[1027,2,256]{2,1,0:T(2,128)(2,1)S(1)} %constant_dynamic-update-slice_fusion, f32[2,256]{1,0:T(2,128)} %get-tuple-element.162, f32[2,256]{1,0:T(2,128)} %get-tuple-element.163, f32[2,256]{1,0:T(2,128)} %get-tuple-element.161, ...), kind=kLoop, calls=%fused_computation.38 | loop fusion | flops 8388608 | bytes 5251072 | tf_op jit(solution)/shard_map/convert_element_type | solution.py:23
  54.2 8.1 %convolution_bitcast_fusion = f32[8,1,32,64,256]{4,3,2,1,0:T(8,128)} fusion(bf16[8,128,32,64]{1,0,3,2:T(8,128)(2,1)S(1)} %multiply_convert_fusion.3, bf16[8,128,2,1,256]{4,1,0,3,2:T(8,128)(2,1)S(1)} %bitcast.135), kind=kOutput, calls=%fused_computation.10 | convolution fusion | flops 1073741824 | bytes 21495808 | tf_op jit(solution)/shard_map/csgjp,csgn->cgjpn/dot_general | solution.py:80
  62.2 27.9 %while.24 = (s32[]{:T(128)}, f32[1,32,64,256]{3,2,1,0:T(8,128)S(1)}, f32[8,1,32,64,256]{4,3,2,1,0:T(8,128)}, f32[8,1,32]{2,1,0:T(1,128)S(1)}, f32[8,1,32,64,256]{4,3,2,1,0:T(8,128)}, /*index=5*/s32[]{:T(128)}, s32[]{:T(128)}) while((s32[]{:T(128)}, f32[1,32,64,256]{3,2,1,0:T(8,128)S(1)}, f32[8,1,32,64,256]{4,3,2,1,0:T(8,128)}, ...), condition=%wide.region_4.5_spmd.clone, body=%wide.region_3.4_spmd.clone.sunk | while | flops 2097155 | bytes 10486752 | solution.py:90
  93.0 33.4 %all-reduce = f32[512]{0:T(512)S(1)} all-reduce(f32[512]{0:T(512)S(1)} %exponential_dynamic-update-slice_fusion), channel_id=2, replica_groups=mesh['ctx'=16,'head'=8] {'ctx'}, use_global_device_ids=true, to_apply=%add | all-reduce | flops 512 | bytes 4096
  126.5 13.3 %reshape.252 = f32[8,128,1,32,64]{4,3,1,0,2:T(8,128)} reshape(bf16[1024,2048]{1,0:T(8,128)(2,1)} %param.14) | data formatting | bytes 12582912 | tf_op jit(solution)/shard_map/convert_element_type | solution.py:119
  139.8 14.5 %copy.46 = f32[8,128,1,32,64]{1,4,3,0,2:T(8,128)} copy(f32[8,128,1,32,64]{4,3,1,0,2:T(8,128)} %reshape.252) | data formatting | bytes 16777216 | tf_op jit(solution)/shard_map/convert_element_type | solution.py:119
  154.4 13.5 %reshape.251 = f32[8,128,1,32,64]{4,3,1,0,2:T(8,128)} reshape(bf16[1024,2048]{1,0:T(8,128)(2,1)} %multiply_convert_fusion.4) | data formatting | bytes 12582912 | tf_op jit(solution)/shard_map/convert_element_type | solution.py:78
  167.9 14.7 %copy.43 = f32[8,128,1,32,64]{1,4,3,0,2:T(8,128)} copy(f32[8,128,1,32,64]{4,3,1,0,2:T(8,128)} %reshape.251) | data formatting | bytes 16777216 | tf_op jit(solution)/shard_map/convert_element_type | solution.py:78
  182.8 11.0 %fusion.3 = f32[8,32,64,128]{3,2,1,0:T(8,128)} fusion(f32[8,32,128]{2,1,0:T(8,128)S(1)} %bitcast.146, f32[8,32,128]{2,1,0:T(8,128)S(1)} %bitcast.139, f32[8,128,128]{2,1,0:T(8,128)S(1)} %fusion.25, pred[128,128]{1,0:T(8,128)(4,1)S(1)} %iota_compare_fusion, bf16[8,128,32,64]{1,0,3,2:T(8,128)(2,1)} %bitcast.131), kind=kOutput, calls=%fused_computation.11 | convolution fusion | flops 557842432 | bytes 13385728 | tf_op jit(solution)/shard_map/cgjts,csgjp->ctgjp/dot_general | solution.py:72
  193.8 97.6 %all-gather.4.cloned.1.call-done = f32[16,32,64,256]{3,2,1,0:T(8,128)} async-done(((f32[1,32,64,256]{3,2,1,0:T(8,128)}), f32[16,32,64,256]{3,2,1,0:T(8,128)}) %all-gather.4.cloned.1.call-update) | async-done | bytes 33554448 | tf_op jit(solution)/shard_map/all_gather | solution.py:95
  291.4 54.1 %while.25 = (s32[]{:T(128)}, f32[1,32,64,256]{3,2,1,0:T(8,128)S(1)}, s32[16]{0:T(128)S(1)}, s32[]{:T(128)}, f32[16,1,32]{2,1,0:T(1,128)S(1)}, /*index=5*/f32[16,1,32,64,256]{4,3,2,1,0:T(8,128)}, s32[]{:T(128)}, s32[]{:T(128)}) while((s32[]{:T(128)}, f32[1,32,64,256]{3,2,1,0:T(8,128)S(1)}, s32[16]{0:T(128)S(1)}, s32[]{:T(128)}, ...), condition=%wide.region_6.7_spmd.clone, body=%wide.region_5.6_spmd.clone.sunk | while | flops 2097156 | bytes 6291965 | solution.py:109
  292.6 2.1 fusion.38
  299.4 2.1 fusion.38
  306.2 2.1 fusion.38
  312.9 2.1 fusion.38
  345.5 11.4 %fusion.5 = f32[8,32,64,128]{3,2,1,0:T(8,128)} fusion(f32[8,1,32,64,256]{4,3,2,1,0:T(8,128)} %get-tuple-element.67, f32[32,64,256]{2,1,0:T(8,128)S(1)} %bitcast.129, f32[8,32]{1,0:T(8,128)S(1)} %subtract_exponential_fusion, bf16[8,128,2,1,256]{4,1,0,3,2:T(8,128)(2,1)S(1)} %bitcast.137), kind=kOutput, calls=%fused_computation.13 | convolution fusion | flops 1086324736 | bytes 27791360 | tf_op jit(solution)/shard_map/ctgn,cgjpn->ctgjp/dot_general | solution.py:113
  356.9 13.1 %multiply_reduce_fusion = (f32[8,128]{1,0:T(8,128)S(1)}, f32[8,128,1,32,64]{1,4,3,0,2:T(8,128)S(1)}) fusion(f32[8,128,1,32,64]{1,4,3,0,2:T(8,128)} %copy.46, f32[8,128,1,32,64]{1,4,3,0,2:T(8,128)} %copy.43, f32[32]{0:T(128)S(1)} %copy-done.6, f32[8,128,32]{1,2,0:T(8,128)S(1)} %copy-done.3, f32[8,32,64,128]{3,2,1,0:T(8,128)} %fusion.5, ...), kind=kLoop, calls=%fused_computation.19 | loop fusion | flops 23067648 | bytes 42078336 | tf_op jit(solution)/shard_map/reduce_sum | solution.py:121
  371.6 54.1 %all_to_all.19 = bf16[8,128,2048]{1,2,0:T(8,128)(2,1)} all-to-all(bf16[8,128,2048]{1,2,0:T(8,128)(2,1)S(1)} %bitcast.130), channel_id=1, replica_groups=mesh['ctx'=16,'head'=8] {'head'}, dimensions={0} | all-to-all | bytes 8388608 | tf_op jit(solution)/shard_map/all_to_all | solution.py:128
  425.7 6.4 %copy.52 = bf16[128,16384]{1,0:T(8,128)(2,1)} copy(bf16[128,16384]{0,1:T(8,128)(2,1)} %bitcast.133) | data formatting | bytes 8388608 | tf_op jit(solution)/shard_map/all_to_all | solution.py:128
  (125 shorter events, 76.5 us)
Async XLA Ops:
  6.5 284.8 %all-gather.4.cloned.1.call-start = ((), (), s32[]{:S(2)}) async-start(), calls=%async_computation.1 | async-start | bytes 35651584 | tf_op jit(solution)/shard_map/all_gather | solution.py:95
  8.0 12.0 %collective-permute-start = (bf16[3,2560]{1,0:T(4,128)(2,1)S(1)}, bf16[3,2560]{1,0:T(4,128)(2,1)S(1)}, u32[]{:S(2)}, u32[]{:S(2)}) collective-permute-start(bf16[3,2560]{1,0:T(4,128)(2,1)S(1)} %pad_maximum_fusion.1), channel_id=1, source_target_pairs={{0,8},{8,16},{16,24},{24,32},{32,40},{40,48},{48,56},{56,64},{64,7... | collective-permute-start | bytes 46088 | tf_op jit(solution)/shard_map/ppermute | solution.py:13
  20.0 0.6 copy-start.4
  34.3 11.7 %slice-start = ((bf16[3,2560]{1,0:T(4,128)(2,1)}), bf16[3,512]{1,0:T(4,128)(2,1)S(1)}, s32[]{:S(2)}) async-start(bf16[3,2560]{1,0:T(4,128)(2,1)} %copy-done.4), calls=%async_computation.2 | async-start | bytes 8192 | tf_op jit(solution)/shard_map/slice | solution.py:51
  34.3 11.8 %copy-start.2 = (bf16[1024,2,256]{2,1,0:T(2,128)(2,1)S(1)}, bf16[1024,2,256]{2,1,0:T(2,128)(2,1)}, u32[]{:S(2)}) copy-start(bf16[1024,2,256]{2,1,0:T(2,128)(2,1)} %param.15) | copy-start | bytes 3145732
  46.0 7.0 %copy-start.1 = (bf16[256,8,8,128]{3,2,1,0:T(8,128)(2,1)S(1)}, bf16[256,8,8,128]{3,2,1,0:T(8,128)(2,1)}, u32[]{:S(2)}) copy-start(bf16[256,8,8,128]{3,2,1,0:T(8,128)(2,1)} %copy.56) | copy-start | bytes 12582916
  62.2 29.4 %copy-start.8 = (u32[128]{0:T(128)S(1)}, u32[128]{0:T(128)}, u32[]{:S(2)}) copy-start(u32[128]{0:T(128)} %constant.57) | copy-start | bytes 1540
  62.2 30.7 %copy-start.7 = (f32[32]{0:T(128)S(1)}, f32[32]{0:T(128)}, u32[]{:S(2)}) copy-start(f32[32]{0:T(128)} %get-tuple-element.128) | copy-start | bytes 388
  90.2 1.3 copy-start
  139.8 14.5 %copy-start.5 = (f32[2048]{0:T(1024)S(1)}, f32[2048]{0:T(1024)}, u32[]{:S(2)}) copy-start(f32[2048]{0:T(1024)} %param.21) | copy-start | bytes 24580
  345.5 11.4 %copy-start.3 = (f32[8,128,32]{1,2,0:T(8,128)S(1)}, f32[8,128,32]{1,2,0:T(8,128)}, u32[]{:S(2)}) copy-start(f32[8,128,32]{1,2,0:T(8,128)} %get-tuple-element.155) | copy-start | bytes 393220
  345.5 11.4 %copy-start.6 = (f32[32]{0:T(128)S(1)}, f32[32]{0:T(128)}, u32[]{:S(2)}) copy-start(f32[32]{0:T(128)} %param.20) | copy-start | bytes 388
Sparse Core Ops, SparseCore 0:
  91.7 199.6 all-gather.3
where the time goes:
time: 442 us; the launch traced here: 439 us
  other arithmetic  103 us (23%)
  waiting for transfers between devices  97.6 us (22%)
  local copies, waits for them, and re-layouts  90.8 us (21%)
  blocking collectives  87.5 us (20%)
  matrix products  30.7 us (7%)
  between operations  14.3 us (3%)
  loops' own time  11.1 us (3%)
    all_gather x1, waiting for transfers between devices, shards(): lax.all_gather(dev_state[None], 'ctx', axis=0, tiled=True)  97.6 us
    all_to_all x1, blocking collectives, shards(): lax.all_to_all(normed, 'head', split_axis=0, concat_axis=1, tiled=True)  54.1 us
    select_n x16, other arithmetic, absorb(): jnp.where(source_rank < my_rank, decay_one[..., None, None] * carried + s...  33.7 us
    unnamed x1, blocking collectives  33.4 us
    convert_element_type x2, local copies, waits for them, and re-layouts, shards(): feat_spans.astype(jnp.float32)  28.1 us
    convert_element_type x2, local copies, waits for them, and re-layouts, shards(): gates.reshape(span_count, SPAN, group_count, per_group, head_dim)  27.8 us
    convert_element_type x2, other arithmetic, conv_rows(): return jax.nn.silu(summed).astype(jnp.bfloat16)  19.6 us
    add x8, other arithmetic, advance(): return (jnp.exp(log_total)[..., None, None] * carried + added, carried)  15.7 us
  transfers between devices with their start and end apart: 2, of which 1 were waited for; matrix products, arithmetic and copies ran while one was open for 17% of the time, Pallas kernels for 0%

commit v1 on v0

v1 whole, which is shorter than its diff:
```python
import functools

import jax
import jax.numpy as jnp
from jax import lax
from jax.experimental import pallas as pl
from jax.experimental.pallas import tpu as pltpu
from jax.sharding import PartitionSpec as P

F32 = jnp.float32
BF16 = jnp.bfloat16
MESH = pl.DeviceIdType.MESH

TOK = 1024
CH = 2048
HEADS = 32
HD = 64
ST = 256
GW = 256
NG = CH // GW
PER = GW // HD
L = 64
NCH = TOK // L
BLK = 128
NB = TOK // BLK
PAD = 16
TAPS = 4


def dot(a, b):
    return jnp.dot(a, b, preferred_element_type=F32)


def dot_nt(a, b):
    return lax.dot_general(a, b, (((1,), (1,)), ((), ())), preferred_element_type=F32)


def silu(v):
    half = 0.5 * v
    return half + half * jnp.tanh(half)


def split3(v):
    hi = v.astype(BF16)
    rest = v - hi.astype(F32)
    mid = rest.astype(BF16)
    low = (rest - mid.astype(F32)).astype(BF16)
    return hi, mid, low


def split_lanes(v):
    hi = v.astype(BF16).astype(F32)
    lane = lax.broadcasted_iota(jnp.int32, v.shape, 1)
    return jnp.where((lane // HEADS) % 2 == 0, hi, v - hi).astype(BF16)


def expander(piece, part):
    row = lax.broadcasted_iota(jnp.int32, (4 * HEADS, GW), 0)
    col = lax.broadcasted_iota(jnp.int32, (4 * HEADS, GW), 1)
    hit = (row % HEADS == PER * piece + col // HD) & (row // (2 * HEADS) == part)
    return jnp.where(hit, 1.0, 0.0).astype(BF16)


def mixer_kernel(
    nc,
    nh,
    feat_hbm,
    gate_hbm,
    sio_hbm,
    step_ref,
    decay_ref,
    cf_ref,
    cs_ref,
    sg_ref,
    z_out,
    rs_out,
    feat,
    gate,
    sio,
    xbuf,
    wx,
    in_rows,
    out_rows,
    in_t4,
    in_t,
    smask,
    fac_ab,
    fac_w,
    rows_fac,
    rows_g,
    shift,
    acc,
    carry,
    sbuf,
    gath,
    pbuf,
    inc,
    dsend,
    dall,
    zsend,
    rs_send,
    feat_sem,
    gate_sem,
    sio_sem,
    halo_send,
    halo_recv,
    d_send_sem,
    d_recv_sem,
    s_send,
    s_recv,
    p_send,
    p_recv,
    z_send,
    z_recv,
    r_send,
    r_recv,
):
    me = lax.axis_index("ctx")
    mh = lax.axis_index("head")
    sl = ST // nc
    tb = TOK // nh
    nxt = lax.rem(me + 1, nc)

    def rank(k):
        return lax.rem(me + k, nc)

    def peer(k):
        return lax.rem(mh + k, nh)

    def sio_in(i):
        return pltpu.make_async_copy(
            sio_hbm.at[i], sio.at[i, pl.ds(PAD, TOK)], sio_sem.at[i]
        )

    def feat_in(g):
        cols = pl.ds(pl.multiple_of(g * GW, GW), GW)
        return pltpu.make_async_copy(
            feat_hbm.at[:, cols], feat.at[g, pl.ds(PAD, TOK)], feat_sem.at[g]
        )

    def gate_in(g):
        cols = pl.ds(pl.multiple_of(g * GW, GW), GW)
        return pltpu.make_async_copy(gate_hbm.at[:, cols], gate.at[g], gate_sem.at[g])

    for i in range(2):
        sio_in(i).start()

    @pl.loop(0, NG)
    def _(g):
        feat_in(g).start()

    @pl.loop(0, NG)
    def _(g):
        gate_in(g).start()

    bar = pltpu.get_barrier_semaphore()

    @pl.loop(1, nc)
    def _(k):
        pl.semaphore_signal(bar, inc=1, device_id={"ctx": rank(k)}, device_id_type=MESH)

    @pl.loop(1, nh)
    def _(k):
        pl.semaphore_signal(bar, inc=1, device_id={"head": peer(k)}, device_id_type=MESH)

    pl.semaphore_wait(bar, nc - 1 + nh - 1)

    def halo_copy(g):
        cols = pl.ds(pl.multiple_of(g * GW, GW), GW)
        return pltpu.make_async_remote_copy(
            src_ref=feat_hbm.at[pl.ds(TOK - PAD, PAD), cols],
            dst_ref=feat.at[g, pl.ds(0, PAD)],
            send_sem=halo_send.at[g],
            recv_sem=halo_recv.at[g],
            device_id={"ctx": nxt},
            device_id_type=MESH,
        )

    def halo_map(i):
        return pltpu.make_async_remote_copy(
            src_ref=sio_hbm.at[i, pl.ds(TOK - PAD, PAD)],
            dst_ref=sio.at[i, pl.ds(0, PAD)],
            send_sem=halo_send.at[NG + i],
            recv_sem=halo_recv.at[NG + i],
            device_id={"ctx": nxt},
            device_id_type=MESH,
        )

    for i in range(2):
        halo_map(i).start()

    @pl.loop(0, NG)
    def _(g):
        halo_copy(g).start()

    def four(v):
        return jnp.concatenate([v, v, v, v], axis=0)

    decay3 = [four(p.astype(F32)).astype(BF16) for p in split3(decay_ref[...])]
    step3 = [four(p.astype(F32)).astype(BF16) for p in split3(step_ref[...])]

    row = lax.broadcasted_iota(jnp.int32, (64, TOK), 0)
    tok = lax.broadcasted_iota(jnp.int32, (64, TOK), 1)
    kind, unit = row // 16, row % 16
    in_chunk = tok // L == unit
    early = tok % L < L // 2
    hit = jnp.where(kind == 0, jnp.where(in_chunk & early, 1.0, 0.0), 0.0)
    hit = hit + jnp.where((kind == 1) & in_chunk, 1.0, 0.0)
    hit = hit + jnp.where((kind == 2) & in_chunk, jnp.where(early, 0.0, 1.0), 0.0)
    hit = hit + jnp.where((kind == 3) & (unit < 8), 1.0, 0.0)
    hit = hit + jnp.where((kind == 3) & (unit >= 8) & (tok // BLK > unit - 8), 1.0, 0.0)
    select = hit.astype(BF16)
    sums = dot_nt(select, decay3[0]) + dot_nt(select, decay3[1]) + dot_nt(select, decay3[2])
    rows_fac[...] = split_lanes(jnp.exp(sums[0:56]))

    r = lax.broadcasted_iota(jnp.int32, (BLK, BLK), 0)
    c = lax.broadcasted_iota(jnp.int32, (BLK, BLK), 1)
    eye = jnp.where(r == c, 1.0, 0.0).astype(BF16)
    after = jnp.where(c > r, 1.0, 0.0).astype(BF16)
    for b in range(NB):
        cut = slice(b * BLK, (b + 1) * BLK)
        suffix = sums[56 + b : 57 + b]
        steps = 0.0
        for d3, s3 in zip(decay3, step3):
            suffix = suffix + dot_nt(after, d3[:, cut])
            steps = steps + dot_nt(eye, s3[:, cut])
        fac_w[cut, :] = split_lanes(jnp.exp(suffix) * steps)

    for g in range(NG):
        spread = dot(rows_fac[48:56, :], expander(g, 0))
        dsend[0, :, g * GW : (g + 1) * GW] = spread[0:1]

    def d_copy(k):
        return pltpu.make_async_remote_copy(
            src_ref=dsend.at[0],
            dst_ref=dall.at[me],
            send_sem=d_send_sem,
            recv_sem=d_recv_sem,
            device_id={"ctx": rank(k)},
            device_id_type=MESH,
        )

    d_own = pltpu.make_async_copy(dsend.at[0], dall.at[me], d_recv_sem)
    d_own.start()

    @pl.loop(1, nc)
    def _(k):
        d_copy(k).start()

    sr = lax.broadcasted_iota(jnp.int32, (BLK, BLK + PAD), 0)
    sc = lax.broadcasted_iota(jnp.int32, (BLK, BLK + PAD), 1)
    for k in range(TAPS):
        shift[k] = jnp.where(sc == sr + PAD - TAPS + 1 + k, 1.0, 0.0).astype(BF16)

    def conv(block, taps):
        total = taps[0:1] * dot(shift[0], block)
        for k in range(1, TAPS):
            total = total + taps[k : k + 1] * dot(shift[k], block)
        return silu(total)

    def maps(i, store):
        sio_in(i).wait()
        halo_map(i).wait()

        @pl.when(me == 0)
        def _():
            sio[i, 0:PAD, :] = jnp.zeros((PAD, ST), BF16)

        taps = cs_ref[i]
        for b in range(NB):
            store(b, conv(sio[i, b * BLK : b * BLK + BLK + PAD, :], taps))

    def store_in(b, v):
        low = v.astype(BF16)
        in_rows[b * BLK : (b + 1) * BLK, :] = low
        turned = low.astype(F32).T.astype(BF16)
        in_t4[:, b * BLK : (b + 1) * BLK] = turned
        in_t[2 * b] = turned[:, 0:L]
        in_t[2 * b + 1] = turned[:, L : 2 * L]

    def store_out(b, v):
        out_rows[b * BLK : (b + 1) * BLK, :] = v.astype(BF16)

    maps(0, store_in)

    def s_copy(g, k):
        return pltpu.make_async_remote_copy(
            src_ref=sbuf.at[g, rank(k)],
            dst_ref=gath.at[g, me],
            send_sem=s_send.at[g],
            recv_sem=s_recv.at[g],
            device_id={"ctx": rank(k)},
            device_id_type=MESH,
        )

    def p_copy(g, k):
        return pltpu.make_async_remote_copy(
            src_ref=pbuf.at[g, rank(k)],
            dst_ref=inc.at[g, me],
            send_sem=p_send.at[g],
            recv_sem=p_recv.at[g],
            device_id={"ctx": rank(k)},
            device_id_type=MESH,
        )

    def z_copy(g, k):
        return pltpu.make_async_remote_copy(
            src_ref=zsend.at[g, peer(k)],
            dst_ref=z_out.at[g, mh],
            send_sem=z_send.at[g],
            recv_sem=z_recv.at[g],
            device_id={"head": peer(k)},
            device_id_type=MESH,
        )

    def phase_a(g):
        feat_in(g).wait()
        halo_copy(g).wait()

        @pl.when(me == 0)
        def _():
            feat[g, 0:PAD, :] = jnp.zeros((PAD, GW), BF16)

        spread = expander(g, 0)
        cols = pl.ds(pl.multiple_of(g * GW, GW), GW)
        taps = cf_ref[:, cols].astype(F32)

        @pl.loop(0, NB)
        def _(b):
            r0 = pl.multiple_of(b * BLK, BLK)
            x = conv(feat[g, pl.ds(r0, BLK + PAD), :], taps).astype(BF16)
            xbuf[g, pl.ds(r0, BLK), :] = x
            w = dot(fac_w[pl.ds(r0, BLK), :], spread)
            wx[pl.ds(r0, BLK), :] = (w * x.astype(F32)).astype(BF16)

        state = dot(in_t4[...], wx[...])
        sbuf[g] = state.astype(BF16).reshape(nc, sl, GW)
        pltpu.make_async_copy(sbuf.at[g, me], gath.at[g, me], s_recv.at[g]).start()

        @pl.loop(1, nc)
        def _(k):
            s_copy(g, k).start()

    def prepare_b():
        maps(1, store_out)
        inside = r // L == c // L
        mid = L // 2 - 1
        plus = inside & (c % L > mid) & (c <= r)
        minus = inside & (c % L <= mid) & (c > r)
        gap = (jnp.where(plus, 1.0, 0.0) - jnp.where(minus, 1.0, 0.0)).astype(BF16)
        lane = lax.broadcasted_iota(jnp.int32, (BLK, BLK), 1)
        for b in range(NB):
            cut = slice(b * BLK, (b + 1) * BLK)
            diff, steps = 0.0, 0.0
            for d3, s3 in zip(decay3, step3):
                diff = diff + dot_nt(gap, d3[:, cut])
                steps = steps + dot_nt(eye, s3[:, cut])
            first = lane < 2 * HEADS
            both = jnp.exp(jnp.where(first, diff, -diff)) * jnp.where(first, 1.0, steps)
            fac_ab[cut, :] = split_lanes(both)
        tr = lax.broadcasted_iota(jnp.int32, (L, L), 0)
        tc = lax.broadcasted_iota(jnp.int32, (L, L), 1)
        for n in range(NCH):
            cut = slice(n * L, (n + 1) * L)
            scores = dot_nt(out_rows[cut, :], in_rows[cut, :])
            smask[n] = jnp.where(tc <= tr, scores, 0.0).astype(BF16)
        acc[...] = jnp.zeros_like(acc)
        whole = dall.at[pl.ds(0, nc)]
        pltpu.make_async_copy(whole, whole, d_recv_sem).wait()

    def phase_x(g):
        pltpu.make_async_copy(gath.at[g], gath.at[g], s_recv.at[g]).wait()
        cols = pl.ds(pl.multiple_of(g * GW, GW), GW)
        running = jnp.zeros((sl, GW), F32)
        for q in range(nc):
            pbuf[g, q] = running.astype(BF16)
            running = dall[q, :, cols] * running + gath[g, q].astype(F32)
        pltpu.make_async_copy(pbuf.at[g, me], inc.at[g, me], p_recv.at[g]).start()

        @pl.loop(1, nc)
        def _(k):
            p_copy(g, k).start()

    def phase_b(g):
        gate_in(g).wait()
        pltpu.make_async_copy(inc.at[g], inc.at[g], p_recv.at[g]).wait()
        spread_a, spread_b = expander(g, 0), expander(g, 1)
        cols = pl.ds(pl.multiple_of(g * GW, GW), GW)
        skip = sg_ref[0:1, cols]
        gain = sg_ref[1:2, cols]
        rows_g[...] = dot(rows_fac[...], spread_a)
        carry[...] = inc[g].reshape(ST, GW).astype(F32)

        @pl.loop(0, NCH)
        def _(n):
            r0 = pl.multiple_of(n * L, L)
            fac = fac_ab[pl.ds(r0, L), :]
            x = xbuf[g, pl.ds(r0, L), :].astype(F32)
            bx = (dot(fac, spread_b) * x).astype(BF16)
            held = carry[...]
            low = (held * rows_g[pl.ds(n, 1), :]).astype(BF16)
            y = dot(smask[n], bx) + dot(out_rows[pl.ds(r0, L), :], low)
            carry[...] = held * rows_g[pl.ds(NCH + n, 1), :] + rows_g[
                pl.ds(2 * NCH + n, 1), :
            ] * dot(in_t[n], bx)
            mixed = dot(fac, spread_a) * y + skip * x
            gated = mixed * silu(gate[g, pl.ds(r0, L), :].astype(F32))
            square = gated * gated
            acc[pl.ds(r0, L), :] += square[:, 0:128] + square[:, 128:256]
            per = tb // L
            zsend[g, n // per, pl.ds(pl.multiple_of((n % per) * L, L), L), :] = (
                gated * gain
            ).astype(BF16)

        pltpu.make_async_copy(zsend.at[g, mh], z_out.at[g, mh], z_recv.at[g]).start()

        @pl.loop(1, nh)
        def _(k):
            z_copy(g, k).start()

    @pl.loop(0, NG + 2)
    def _(i):
        @pl.when(i < NG)
        def _():
            phase_a(i)

        @pl.when(i == 1)
        def _():
            prepare_b()

        @pl.when((i >= 1) & (i < NG + 1))
        def _():
            phase_x(i - 1)

        @pl.when(i >= 2)
        def _():
            phase_b(i - 2)

    for b in range(NB):
        flat = jnp.sum(acc[b * BLK : (b + 1) * BLK, :].T, axis=0, keepdims=True)
        unit, part = b * BLK // tb, b * BLK % tb
        rs_send[unit, :, part : part + BLK] = lax.rsqrt(flat * (1.0 / CH) + 1e-05)
    pltpu.make_async_copy(rs_send.at[mh], rs_out.at[mh], r_recv).start()

    def r_copy(k):
        return pltpu.make_async_remote_copy(
            src_ref=rs_send.at[peer(k)],
            dst_ref=rs_out.at[mh],
            send_sem=r_send,
            recv_sem=r_recv,
            device_id={"head": peer(k)},
            device_id_type=MESH,
        )

    @pl.loop(1, nh)
    def _(k):
        r_copy(k).start()

    some = dall.at[pl.ds(0, nc - 1)]
    pltpu.make_async_copy(some, some, d_send_sem).wait()

    @pl.loop(0, NG)
    def _(g):
        part = gath.at[g, pl.ds(0, nc - 1)]
        pltpu.make_async_copy(part, part, s_send.at[g]).wait()
        pltpu.make_async_copy(part, part, p_send.at[g]).wait()
        piece = zsend.at[g, pl.ds(0, nh - 1)]
        pltpu.make_async_copy(piece, piece, z_send.at[g]).wait()

    @pl.loop(0, NG)
    def _(g):
        pltpu.make_async_copy(zsend.at[g], zsend.at[g], z_recv.at[g]).wait()

    part = rs_send.at[pl.ds(0, nh - 1)]
    pltpu.make_async_copy(part, part, r_send).wait()
    pltpu.make_async_copy(rs_send, rs_send, r_recv).wait()


def mixer(nc, nh, features, gates, sio, step_size, log_decay, conv_feat, taps_io, sg):
    sl, tb = ST // nc, TOK // nh
    any_spec = pl.BlockSpec(memory_space=pl.ANY)
    vmem = pl.BlockSpec(memory_space=pltpu.VMEM)
    dma = pltpu.SemaphoreType.DMA
    return pl.pallas_call(
        functools.partial(mixer_kernel, nc, nh),
        out_shape=[
            jax.ShapeDtypeStruct((NG, nh, tb, GW), BF16),
            jax.ShapeDtypeStruct((nh, 1, tb), F32),
        ],
        in_specs=[any_spec] * 3 + [vmem] * 5,
        out_specs=[any_spec, any_spec],
        scratch_shapes=[
            pltpu.VMEM((NG, TOK + PAD, GW), BF16),
            pltpu.VMEM((NG, TOK, GW), BF16),
            pltpu.VMEM((2, TOK + PAD, ST), BF16),
            pltpu.VMEM((NG, TOK, GW), BF16),
            pltpu.VMEM((TOK, GW), BF16),
            pltpu.VMEM((TOK, ST), BF16),
            pltpu.VMEM((TOK, ST), BF16),
            pltpu.VMEM((ST, TOK), BF16),
            pltpu.VMEM((NCH, ST, L), BF16),
            pltpu.VMEM((NCH, L, L), BF16),
            pltpu.VMEM((TOK, 128), BF16),
            pltpu.VMEM((TOK, 128), BF16),
            pltpu.VMEM((56, 128), BF16),
            pltpu.VMEM((56, GW), F32),
            pltpu.VMEM((TAPS, BLK, BLK + PAD), BF16),
            pltpu.VMEM((TOK, 128), F32),
            pltpu.VMEM((ST, GW), F32),
            pltpu.VMEM((NG, nc, sl, GW), BF16),
            pltpu.VMEM((NG, nc, sl, GW), BF16),
            pltpu.VMEM((NG, nc, sl, GW), BF16),
            pltpu.VMEM((NG, nc, sl, GW), BF16),
            pltpu.VMEM((1, 1, CH), F32),
            pltpu.VMEM((nc, 1, CH), F32),
            pltpu.VMEM((NG, nh, tb, GW), BF16),
            pltpu.VMEM((nh, 1, tb), F32),
            dma((NG,)),
            dma((NG,)),
            dma((2,)),
            dma((NG + 2,)),
            dma((NG + 2,)),
            dma,
            dma,
            dma((NG,)),
            dma((NG,)),
            dma((NG,)),
            dma((NG,)),
            dma((NG,)),
            dma((NG,)),
            dma,
            dma,
        ],
        compiler_params=pltpu.CompilerParams(
            collective_id=0, has_side_effects=True, vmem_limit_bytes=52 << 20
        ),
        cost_estimate=pl.CostEstimate(
            flops=6_000_000_000, bytes_accessed=16_000_000, transcendentals=5_000_000
        ),
    )(features, gates, sio, step_size, log_decay, conv_feat, taps_io, sg)


def norm_kernel(z_ref, rs_ref, o_ref):
    tb = z_ref.shape[2]
    rows = jnp.broadcast_to(rs_ref[0], (128, tb))
    col = rows.T
    both = jnp.concatenate([col, col], axis=1)
    for g in range(NG):
        o_ref[:, g * GW : (g + 1) * GW] = (z_ref[g, 0].astype(F32) * both).astype(BF16)


def normalize(nh, z, rs):
    tb = TOK // nh
    return pl.pallas_call(
        norm_kernel,
        grid=(nh,),
        out_shape=jax.ShapeDtypeStruct((tb, nh * CH), BF16),
        in_specs=[
            pl.BlockSpec((NG, 1, tb, GW), lambda j: (0, j, 0, 0)),
            pl.BlockSpec((1, 1, tb), lambda j: (j, 0, 0)),
        ],
        out_specs=pl.BlockSpec((tb, CH), lambda j: (0, j)),
        cost_estimate=pl.CostEstimate(
            flops=4_000_000, bytes_accessed=8_400_000, transcendentals=0
        ),
    )(z, rs)


def shards(
    features, gates, state_io, step_size, log_decay, conv_feat, conv_state, skip_gain, norm_gain
):
    nc, nh = lax.axis_size("ctx"), lax.axis_size("head")
    sio = jnp.transpose(state_io, (1, 0, 2))
    taps_io = jnp.transpose(conv_state, (1, 0, 2)).astype(F32)
    sg = jnp.stack([jnp.repeat(skip_gain, HD), norm_gain])
    z, rs = mixer(nc, nh, features, gates, sio, step_size, log_decay, conv_feat, taps_io, sg)
    return normalize(nh, z, rs)


def solution(mesh):
    in_specs = (
        P("ctx", "head"),
        P("ctx", "head"),
        P("ctx", None, "head"),
        P("head", "ctx"),
        P("head", "ctx"),
        P(None, "head"),
        P(None, None, "head"),
        P("head"),
        P("head"),
    )
    out_specs = P(("ctx", "head"), None)
    return jax.shard_map(shards, mesh=mesh, in_specs=in_specs, out_specs=out_specs, check_vma=False)
```

time: 442 us -> 107 us (0.24)
  other arithmetic: 103 us -> 1.41 us
  Pallas kernels: 0 us -> 99.5 us
  waiting for transfers between devices: 97.6 us -> 0 us
  blocking collectives: 87.5 us -> 0 us
  local copies, waits for them, and re-layouts: 90.8 us -> 5.28 us
  matrix products: 30.7 us -> 0 us
  between operations: 14.3 us -> 0.03 us
  loops' own time: 11.1 us -> 0 us
    pallas_call x0 -> x2, Pallas kernels: none -> 99.5 us  [the longest x1 92.5 us: mixer(): pl.pallas_call(functools.partial(mixer_kernel, nc, nh), out_shape=[jax.Sh...]
    all_gather x1 -> x0, waiting for transfers between devices: 97.6 us -> none  [shards(): lax.all_gather(dev_state[None], 'ctx', axis=0, tiled=True)]
    convert_element_type x6 -> x0, local copies, waits for them, and re-layouts: 62.5 us -> none  [the longest x2 28.1 us: shards(): feat_spans.astype(jnp.float32)]
    all_to_all x1 -> x0, blocking collectives: 54.1 us -> none  [shards(): lax.all_to_all(normed, 'head', split_axis=0, concat_axis=1, tiled=True)]
    select_n x16 -> x0, other arithmetic: 33.7 us -> none  [absorb(): jnp.where(source_rank < my_rank, decay_one[..., None, None] * carried + s...]
    unnamed x1 -> x0, blocking collectives: 33.4 us -> none
    dot_general x4 -> x0, matrix products: 30.7 us -> none  [the longest x1 11.4 us: shards(): jnp.einsum('ctgn,cgjpn->ctgjp', out_maps, state_low, preferred_element_ty...]
    convert_element_type x4 -> x1, other arithmetic: 22.3 us -> 0.69 us  [shards(): taps_io = jnp.transpose(conv_state, (1, 0, 2)).astype(F32)]
  transfers between devices with their start and end apart: 2 -> 0, of which waited for: 1 -> 0; matrix products, arithmetic and copies ran while one was open for 17% -> 0% of each run, Pallas kernels for 0% -> 0%
where the time goes in v1:
time: 107 us; the launch traced here: 106 us
  Pallas kernels  99.5 us (93%)
  local copies, waits for them, and re-layouts  5.28 us (5%)
  other arithmetic  1.41 us (1%)
    pallas_call x1, Pallas kernels, mixer(): pl.pallas_call(functools.partial(mixer_kernel, nc, nh), out_shape=[jax.Sh...  92.5 us
    pallas_call x1, Pallas kernels, normalize(): pl.pallas_call(norm_kernel, grid=(nh,), out_shape=jax.ShapeDtypeStruct((t...  7.05 us
    unnamed x9, local copies, waits for them, and re-layouts  4.47 us

profile of v1, /device:TPU:1, one launch (start us, length us, event | category | flops | bytes accessed | tf_op | source)
XLA Modules:
  0.0 106.2 jit_solution(10052396963440204685)
XLA Ops:
  0.0 0.7 convert_bitcast_fusion.cs_ref
  0.7 0.7 broadcast_in_dim.3
  1.4 0.1 stack_reshape.3
  1.5 0.7 pad_maximum_fusion.sg_ref
  2.2 1.4 %copy.14 = bf16[1024,2,256]{2,0,1:T(8,128)(2,1)S(1)} copy(bf16[1024,2,256]{2,1,0:T(2,128)(2,1)} %param.11) | data formatting | bytes 2097152 | tf_op args[2]
  3.6 0.0 copy-start.1
  3.6 0.9 copy-done.1
  4.5 0.0 copy-start.2
  4.5 0.9 copy-done.2
  5.4 0.0 copy-start.3
  5.4 0.7 copy-done.3
  6.1 92.5 %shard_map.91 = (bf16[8,8,128,256]{3,2,1,0:T(8,128)(2,1)}, f32[8,1,128]{2,1,0:T(1,128)S(1)}) custom-call(bf16[1024,2048]{1,0:T(8,128)(2,1)} %feat_hbm.1, bf16[1024,2048]{1,0:T(8,128)(2,1)} %gate_hbm.1, bf16[2,1024,256]{2,1,0:T(8,128)(2,1)S(1)} %bitcast.6, f32[32,1024]{1,0:T(8,128)S(1)} %copy-done.1, f32[32,1024]{1,0:T(8,128)S(1)} %copy-done.2, ...), custom_call_target="tpu_custom_call" | custom-call | flops 6000000000 | bytes 16000000 | tf_op jit(solution)/shard_map/pallas_call | solution.py:484
  98.6 0.0 copy-start
  98.6 0.6 copy-done
  99.2 7.0 %shard_map.92 = bf16[128,16384]{1,0:T(8,128)(2,1)} custom-call(bf16[8,8,128,256]{3,2,1,0:T(8,128)(2,1)} %get-tuple-element.7.z_ref, f32[8,1,128]{2,1,0:T(1,128)} %copy-done), custom_call_target="tpu_custom_call" | custom-call | flops 4000000 | bytes 8400000 | tf_op jit(solution)/shard_map/pallas_call | solution.py:554
Async XLA Ops:
  3.6 0.9 copy-start.1
  4.5 0.9 copy-start.2
  5.4 0.7 copy-start.3
  98.6 0.6 copy-start

commit v2 on v1

--- a/solution.py
+++ b/solution.py
@@ -20,7 +20,6 @@
 NG = CH // GW
 PER = GW // HD
 L = 64
-NCH = TOK // L
 BLK = 128
 NB = TOK // BLK
 PAD = 16
@@ -67,13 +66,21 @@
     feat_hbm,
     gate_hbm,
     sio_hbm,
+    step_hbm,
+    decay_hbm,
+    cf_hbm,
+    cs_hbm,
+    skip_hbm,
+    gain_hbm,
+    z_out,
+    rs_out,
     step_ref,
     decay_ref,
     cf_ref,
     cs_ref,
-    sg_ref,
-    z_out,
-    rs_out,
+    skip_ref,
+    gain_ref,
+    skip_row,
     feat,
     gate,
     sio,
@@ -82,7 +89,6 @@
     in_rows,
     out_rows,
     in_t4,
-    in_t,
     smask,
     fac_ab,
     fac_w,
@@ -99,6 +105,7 @@
     dall,
     zsend,
     rs_send,
+    small_sem,
     feat_sem,
     gate_sem,
     sio_sem,
@@ -142,6 +149,21 @@
         cols = pl.ds(pl.multiple_of(g * GW, GW), GW)
         return pltpu.make_async_copy(gate_hbm.at[:, cols], gate.at[g], gate_sem.at[g])
 
+    small = [
+        pltpu.make_async_copy(source, target, small_sem.at[i])
+        for i, (source, target) in enumerate(
+            [
+                (decay_hbm, decay_ref),
+                (step_hbm, step_ref),
+                (cs_hbm, cs_ref),
+                (cf_hbm, cf_ref),
+                (skip_hbm, skip_ref),
+                (gain_hbm, gain_ref),
+            ]
+        )
+    ]
+    for copy in small:
+        copy.start()
     for i in range(2):
         sio_in(i).start()
 
@@ -149,10 +171,6 @@
     def _(g):
         feat_in(g).start()
 
-    @pl.loop(0, NG)
-    def _(g):
-        gate_in(g).start()
-
     bar = pltpu.get_barrier_semaphore()
 
     @pl.loop(1, nc)
@@ -163,7 +181,8 @@
     def _(k):
         pl.semaphore_signal(bar, inc=1, device_id={"head": peer(k)}, device_id_type=MESH)
 
-    pl.semaphore_wait(bar, nc - 1 + nh - 1)
+    for copy in small:
+        copy.wait()
 
     def halo_copy(g):
         cols = pl.ds(pl.multiple_of(g * GW, GW), GW)
@@ -186,13 +205,6 @@
             device_id_type=MESH,
         )
 
-    for i in range(2):
-        halo_map(i).start()
-
-    @pl.loop(0, NG)
-    def _(g):
-        halo_copy(g).start()
-
     def four(v):
         return jnp.concatenate([v, v, v, v], axis=0)
 
@@ -201,14 +213,18 @@
 
     row = lax.broadcasted_iota(jnp.int32, (64, TOK), 0)
     tok = lax.broadcasted_iota(jnp.int32, (64, TOK), 1)
-    kind, unit = row // 16, row % 16
-    in_chunk = tok // L == unit
-    early = tok % L < L // 2
-    hit = jnp.where(kind == 0, jnp.where(in_chunk & early, 1.0, 0.0), 0.0)
-    hit = hit + jnp.where((kind == 1) & in_chunk, 1.0, 0.0)
-    hit = hit + jnp.where((kind == 2) & in_chunk, jnp.where(early, 0.0, 1.0), 0.0)
-    hit = hit + jnp.where((kind == 3) & (unit < 8), 1.0, 0.0)
-    hit = hit + jnp.where((kind == 3) & (unit >= 8) & (tok // BLK > unit - 8), 1.0, 0.0)
+    kind, unit = row // 8, row % 8
+    chunk = row % 16
+    late = tok % BLK >= L // 2 + L * (chunk % 2)
+    own = tok // BLK == chunk // 2
+    whole = tok // BLK == unit
+    middle = (tok % BLK >= L // 2) & (tok % BLK < L // 2 + L)
+    hit = jnp.where((kind < 2) & own, jnp.where(late, 0.0, 1.0), 0.0)
+    hit = hit + jnp.where((kind >= 2) & (kind < 4) & own & late, 1.0, 0.0)
+    hit = hit + jnp.where((kind == 4) & whole, 1.0, 0.0)
+    hit = hit + jnp.where((kind == 5) & whole & middle, 1.0, 0.0)
+    hit = hit + jnp.where(kind == 6, 1.0, 0.0)
+    hit = hit + jnp.where((kind == 7) & (tok // BLK > unit), 1.0, 0.0)
     select = hit.astype(BF16)
     sums = dot_nt(select, decay3[0]) + dot_nt(select, decay3[1]) + dot_nt(select, decay3[2])
     rows_fac[...] = split_lanes(jnp.exp(sums[0:56]))
@@ -226,9 +242,28 @@
             steps = steps + dot_nt(eye, s3[:, cut])
         fac_w[cut, :] = split_lanes(jnp.exp(suffix) * steps)
 
-    for g in range(NG):
-        spread = dot(rows_fac[48:56, :], expander(g, 0))
-        dsend[0, :, g * GW : (g + 1) * GW] = spread[0:1]
+    head = lax.broadcasted_iota(jnp.int32, (HEADS, CH), 0)
+    chan = lax.broadcasted_iota(jnp.int32, (HEADS, CH), 1)
+    widen = jnp.where(chan // HD == head, 1.0, 0.0).astype(BF16)
+
+    def widened(v):
+        hi, mid, low = split3(v)
+        return dot(hi, widen) + dot(mid, widen) + dot(low, widen)
+
+    dsend[0] = widened(jnp.exp(sums[48:56, 0:HEADS]))[0:1]
+    skip_row[...] = widened(jnp.broadcast_to(skip_ref[...], (8, HEADS)))[0:1]
+
+    pl.semaphore_wait(bar, nc - 1 + nh - 1)
+    for i in range(2):
+        halo_map(i).start()
+
+    @pl.loop(0, NG)
+    def _(g):
+        halo_copy(g).start()
+
+    @pl.loop(0, NG)
+    def _(g):
+        gate_in(g).start()
 
     def d_copy(k):
         return pltpu.make_async_remote_copy(
@@ -249,34 +284,37 @@
 
     sr = lax.broadcasted_iota(jnp.int32, (BLK, BLK + PAD), 0)
     sc = lax.broadcasted_iota(jnp.int32, (BLK, BLK + PAD), 1)
-    for k in range(TAPS):
+    for k in range(TAPS - 1):
         shift[k] = jnp.where(sc == sr + PAD - TAPS + 1 + k, 1.0, 0.0).astype(BF16)
 
     def conv(block, taps):
-        total = taps[0:1] * dot(shift[0], block)
-        for k in range(1, TAPS):
+        total = taps[TAPS - 1 : TAPS] * block[PAD:, :].astype(F32)
+        for k in range(TAPS - 1):
             total = total + taps[k : k + 1] * dot(shift[k], block)
         return silu(total)
 
     def maps(i, store):
         sio_in(i).wait()
+        taps = cs_ref[...].astype(F32)[:, i]
+
+        def one(b):
+            store(b, conv(sio[i, b * BLK : b * BLK + BLK + PAD, :], taps))
+
+        for b in range(1, NB):
+            one(b)
         halo_map(i).wait()
 
         @pl.when(me == 0)
         def _():
             sio[i, 0:PAD, :] = jnp.zeros((PAD, ST), BF16)
 
-        taps = cs_ref[i]
-        for b in range(NB):
-            store(b, conv(sio[i, b * BLK : b * BLK + BLK + PAD, :], taps))
+        one(0)
 
     def store_in(b, v):
         low = v.astype(BF16)
         in_rows[b * BLK : (b + 1) * BLK, :] = low
         turned = low.astype(F32).T.astype(BF16)
         in_t4[:, b * BLK : (b + 1) * BLK] = turned
-        in_t[2 * b] = turned[:, 0:L]
-        in_t[2 * b + 1] = turned[:, L : 2 * L]
 
     def store_out(b, v):
         out_rows[b * BLK : (b + 1) * BLK, :] = v.astype(BF16)
@@ -315,24 +353,25 @@
 
     def phase_a(g):
         feat_in(g).wait()
+        spread = expander(g, 0)
+        cols = pl.ds(pl.multiple_of(g * GW, GW), GW)
+        taps = cf_ref[:, cols].astype(F32)
+
+        def one(b):
+            cut = slice(b * BLK, (b + 1) * BLK)
+            x = conv(feat[g, b * BLK : b * BLK + BLK + PAD, :], taps).astype(BF16)
+            xbuf[g, cut, :] = x
+            wx[cut, :] = (dot(fac_w[cut, :], spread) * x.astype(F32)).astype(BF16)
+
+        for b in range(1, NB):
+            one(b)
         halo_copy(g).wait()
 
         @pl.when(me == 0)
         def _():
             feat[g, 0:PAD, :] = jnp.zeros((PAD, GW), BF16)
 
-        spread = expander(g, 0)
-        cols = pl.ds(pl.multiple_of(g * GW, GW), GW)
-        taps = cf_ref[:, cols].astype(F32)
-
-        @pl.loop(0, NB)
-        def _(b):
-            r0 = pl.multiple_of(b * BLK, BLK)
-            x = conv(feat[g, pl.ds(r0, BLK + PAD), :], taps).astype(BF16)
-            xbuf[g, pl.ds(r0, BLK), :] = x
-            w = dot(fac_w[pl.ds(r0, BLK), :], spread)
-            wx[pl.ds(r0, BLK), :] = (w * x.astype(F32)).astype(BF16)
-
+        one(0)
         state = dot(in_t4[...], wx[...])
         sbuf[g] = state.astype(BF16).reshape(nc, sl, GW)
         pltpu.make_async_copy(sbuf.at[g, me], gath.at[g, me], s_recv.at[g]).start()
@@ -358,12 +397,10 @@
             first = lane < 2 * HEADS
             both = jnp.exp(jnp.where(first, diff, -diff)) * jnp.where(first, 1.0, steps)
             fac_ab[cut, :] = split_lanes(both)
-        tr = lax.broadcasted_iota(jnp.int32, (L, L), 0)
-        tc = lax.broadcasted_iota(jnp.int32, (L, L), 1)
-        for n in range(NCH):
-            cut = slice(n * L, (n + 1) * L)
+        for n in range(NB):
+            cut = slice(n * BLK, (n + 1) * BLK)
             scores = dot_nt(out_rows[cut, :], in_rows[cut, :])
-            smask[n] = jnp.where(tc <= tr, scores, 0.0).astype(BF16)
+            smask[n] = jnp.where(c <= r, scores, 0.0).astype(BF16)
         acc[...] = jnp.zeros_like(acc)
         whole = dall.at[pl.ds(0, nc)]
         pltpu.make_async_copy(whole, whole, d_recv_sem).wait()
@@ -386,29 +423,44 @@
         pltpu.make_async_copy(inc.at[g], inc.at[g], p_recv.at[g]).wait()
         spread_a, spread_b = expander(g, 0), expander(g, 1)
         cols = pl.ds(pl.multiple_of(g * GW, GW), GW)
-        skip = sg_ref[0:1, cols]
-        gain = sg_ref[1:2, cols]
+        skip = skip_row[:, cols]
+        gain = gain_ref[:, cols]
         rows_g[...] = dot(rows_fac[...], spread_a)
         carry[...] = inc[g].reshape(ST, GW).astype(F32)
 
-        @pl.loop(0, NCH)
+        @pl.loop(0, NB, unroll=2)
         def _(n):
-            r0 = pl.multiple_of(n * L, L)
-            fac = fac_ab[pl.ds(r0, L), :]
-            x = xbuf[g, pl.ds(r0, L), :].astype(F32)
-            bx = (dot(fac, spread_b) * x).astype(BF16)
+            r0 = pl.multiple_of(n * BLK, BLK)
+
+            def factor(i):
+                return rows_g[pl.ds(i, 1), :]
+
+            fac = fac_ab[pl.ds(r0, BLK), :]
+            x = xbuf[g, pl.ds(r0, BLK), :].astype(F32)
+            both = dot(fac, spread_b) * x
+            early, late = both[0:L], both[L:BLK]
+            to_late = jnp.concatenate([early * factor(40 + n), late], axis=0)
+            to_end = jnp.concatenate(
+                [early * factor(16 + 2 * n), late * factor(17 + 2 * n)], axis=0
+            )
             held = carry[...]
-            low = (held * rows_g[pl.ds(n, 1), :]).astype(BF16)
-            y = dot(smask[n], bx) + dot(out_rows[pl.ds(r0, L), :], low)
-            carry[...] = held * rows_g[pl.ds(NCH + n, 1), :] + rows_g[
-                pl.ds(2 * NCH + n, 1), :
-            ] * dot(in_t[n], bx)
+            carried = dot(out_rows[pl.ds(r0, BLK), :], held.astype(BF16))
+            added = dot(in_t4[:, pl.ds(r0, BLK)], to_end.astype(BF16))
+            carry[...] = held * factor(32 + n) + added
+            y = jnp.concatenate(
+                [
+                    dot(smask[n, 0:L, 0:L], early.astype(BF16)) + carried[0:L] * factor(2 * n),
+                    dot(smask[n, L:BLK, :], to_late.astype(BF16))
+                    + carried[L:BLK] * factor(2 * n + 1),
+                ],
+                axis=0,
+            )
             mixed = dot(fac, spread_a) * y + skip * x
-            gated = mixed * silu(gate[g, pl.ds(r0, L), :].astype(F32))
+            gated = mixed * silu(gate[g, pl.ds(r0, BLK), :].astype(F32))
             square = gated * gated
-            acc[pl.ds(r0, L), :] += square[:, 0:128] + square[:, 128:256]
-            per = tb // L
-            zsend[g, n // per, pl.ds(pl.multiple_of((n % per) * L, L), L), :] = (
+            acc[pl.ds(r0, BLK), :] += square[:, 0:128] + square[:, 128:256]
+            per = tb // BLK
+            zsend[g, n // per, pl.ds(pl.multiple_of((n % per) * BLK, BLK), BLK), :] = (
                 gated * gain
             ).astype(BF16)
 
@@ -476,10 +528,10 @@
     pltpu.make_async_copy(rs_send, rs_send, r_recv).wait()
 
 
-def mixer(nc, nh, features, gates, sio, step_size, log_decay, conv_feat, taps_io, sg):
+def mixer(nc, nh, *args):
     sl, tb = ST // nc, TOK // nh
     any_spec = pl.BlockSpec(memory_space=pl.ANY)
-    vmem = pl.BlockSpec(memory_space=pltpu.VMEM)
+    hbm = pl.BlockSpec(memory_space=pltpu.HBM)
     dma = pltpu.SemaphoreType.DMA
     return pl.pallas_call(
         functools.partial(mixer_kernel, nc, nh),
@@ -487,9 +539,16 @@
             jax.ShapeDtypeStruct((NG, nh, tb, GW), BF16),
             jax.ShapeDtypeStruct((nh, 1, tb), F32),
         ],
-        in_specs=[any_spec] * 3 + [vmem] * 5,
+        in_specs=[any_spec] * 3 + [hbm] * 6,
         out_specs=[any_spec, any_spec],
         scratch_shapes=[
+            pltpu.VMEM((HEADS, TOK), F32),
+            pltpu.VMEM((HEADS, TOK), F32),
+            pltpu.VMEM((TAPS, CH), BF16),
+            pltpu.VMEM((TAPS, 2, ST), BF16),
+            pltpu.VMEM((1, HEADS), F32),
+            pltpu.VMEM((1, CH), F32),
+            pltpu.VMEM((1, CH), F32),
             pltpu.VMEM((NG, TOK + PAD, GW), BF16),
             pltpu.VMEM((NG, TOK, GW), BF16),
             pltpu.VMEM((2, TOK + PAD, ST), BF16),
@@ -498,13 +557,12 @@
             pltpu.VMEM((TOK, ST), BF16),
             pltpu.VMEM((TOK, ST), BF16),
             pltpu.VMEM((ST, TOK), BF16),
-            pltpu.VMEM((NCH, ST, L), BF16),
-            pltpu.VMEM((NCH, L, L), BF16),
+            pltpu.VMEM((NB, BLK, BLK), BF16),
             pltpu.VMEM((TOK, 128), BF16),
             pltpu.VMEM((TOK, 128), BF16),
             pltpu.VMEM((56, 128), BF16),
             pltpu.VMEM((56, GW), F32),
-            pltpu.VMEM((TAPS, BLK, BLK + PAD), BF16),
+            pltpu.VMEM((TAPS - 1, BLK, BLK + PAD), BF16),
             pltpu.VMEM((TOK, 128), F32),
             pltpu.VMEM((ST, GW), F32),
             pltpu.VMEM((NG, nc, sl, GW), BF16),
@@ -515,6 +573,7 @@
             pltpu.VMEM((nc, 1, CH), F32),
             pltpu.VMEM((NG, nh, tb, GW), BF16),
             pltpu.VMEM((nh, 1, tb), F32),
+            dma((6,)),
             dma((NG,)),
             dma((NG,)),
             dma((2,)),
@@ -532,34 +591,67 @@
             dma,
         ],
         compiler_params=pltpu.CompilerParams(
-            collective_id=0, has_side_effects=True, vmem_limit_bytes=52 << 20
+            collective_id=0, has_side_effects=True, vmem_limit_bytes=56 << 20
         ),
         cost_estimate=pl.CostEstimate(
             flops=6_000_000_000, bytes_accessed=16_000_000, transcendentals=5_000_000
         ),
-    )(features, gates, sio, step_size, log_decay, conv_feat, taps_io, sg)
-
-
-def norm_kernel(z_ref, rs_ref, o_ref):
-    tb = z_ref.shape[2]
-    rows = jnp.broadcast_to(rs_ref[0], (128, tb))
-    col = rows.T
-    both = jnp.concatenate([col, col], axis=1)
-    for g in range(NG):
-        o_ref[:, g * GW : (g + 1) * GW] = (z_ref[g, 0].astype(F32) * both).astype(BF16)
+    )(*args)
+
+
+def norm_kernel(z_hbm, rs_hbm, o_hbm, zin, rs, stage, in_sem, rs_sem, out_sem):
+    nh, tb = z_hbm.shape[1], z_hbm.shape[2]
+
+    def into(j):
+        return pltpu.make_async_copy(z_hbm.at[:, j], zin.at[j], in_sem.at[j])
+
+    def out(j):
+        cols = pl.ds(pl.multiple_of(j * CH, CH), CH)
+        return pltpu.make_async_copy(stage.at[j], o_hbm.at[:, cols], out_sem.at[j])
+
+    factors = pltpu.make_async_copy(rs_hbm, rs, rs_sem)
+    factors.start()
+
+    @pl.loop(0, nh)
+    def _(j):
+        into(j).start()
+
+    factors.wait()
+
+    @pl.loop(0, nh)
+    def _(j):
+        col = jnp.broadcast_to(rs[j], (128, tb)).T
+        into(j).wait()
+        for g in range(NG):
+            for half in range(GW // 128):
+                low = half * 128
+                z = zin[j, g, :, low : low + 128].astype(F32)
+                stage[j, :, g * GW + low : g * GW + low + 128] = (z * col).astype(BF16)
+        out(j).start()
+
+    @pl.loop(0, nh)
+    def _(j):
+        out(j).wait()
 
 
 def normalize(nh, z, rs):
     tb = TOK // nh
+    hbm = pl.BlockSpec(memory_space=pltpu.HBM)
+    dma = pltpu.SemaphoreType.DMA
     return pl.pallas_call(
         norm_kernel,
-        grid=(nh,),
         out_shape=jax.ShapeDtypeStruct((tb, nh * CH), BF16),
-        in_specs=[
-            pl.BlockSpec((NG, 1, tb, GW), lambda j: (0, j, 0, 0)),
-            pl.BlockSpec((1, 1, tb), lambda j: (j, 0, 0)),
+        in_specs=[hbm, hbm],
+        out_specs=hbm,
+        scratch_shapes=[
+            pltpu.VMEM((nh, NG, tb, GW), BF16),
+            pltpu.VMEM((nh, 1, tb), F32),
+            pltpu.VMEM((nh, tb, CH), BF16),
+            dma((nh,)),
+            dma,
+            dma((nh,)),
         ],
-        out_specs=pl.BlockSpec((tb, CH), lambda j: (0, j)),
+        compiler_params=pltpu.CompilerParams(vmem_limit_bytes=56 << 20),
         cost_estimate=pl.CostEstimate(
             flops=4_000_000, bytes_accessed=8_400_000, transcendentals=0
         ),
@@ -571,9 +663,19 @@
 ):
     nc, nh = lax.axis_size("ctx"), lax.axis_size("head")
     sio = jnp.transpose(state_io, (1, 0, 2))
-    taps_io = jnp.transpose(conv_state, (1, 0, 2)).astype(F32)
-    sg = jnp.stack([jnp.repeat(skip_gain, HD), norm_gain])
-    z, rs = mixer(nc, nh, features, gates, sio, step_size, log_decay, conv_feat, taps_io, sg)
+    z, rs = mixer(
+        nc,
+        nh,
+        features,
+        gates,
+        sio,
+        step_size,
+        log_decay,
+        conv_feat,
+        conv_state,
+        skip_gain.reshape(1, HEADS),
+        norm_gain.reshape(1, CH),
+    )
     return normalize(nh, z, rs)
 
 

time: 107 us -> 80.7 us (0.75)
  Pallas kernels: 99.5 us -> 78.2 us
  local copies, waits for them, and re-layouts: 5.28 us -> 2.33 us
  other arithmetic: 1.41 us -> 0 us
    pallas_call x1, Pallas kernels: 92.5 us -> 74.3 us  [mixer(): pl.pallas_call(functools.partial(mixer_kernel, nc, nh), out_shape=[jax.Sh...]
    pallas_call x1, Pallas kernels: 7.05 us -> 3.86 us  [normalize(): pl.pallas_call(norm_kernel, out_shape=jax.ShapeDtypeStruct((tb, nh * CH),...]
    unnamed x9 -> x1, local copies, waits for them, and re-layouts: 4.47 us -> 2.33 us
where the time goes in v2:
time: 80.7 us; the launch traced here: 80.5 us
  Pallas kernels  78.2 us (97%)
  local copies, waits for them, and re-layouts  2.33 us (3%)
    pallas_call x1, Pallas kernels, mixer(): pl.pallas_call(functools.partial(mixer_kernel, nc, nh), out_shape=[jax.Sh...  74.3 us
    pallas_call x1, Pallas kernels, normalize(): pl.pallas_call(norm_kernel, out_shape=jax.ShapeDtypeStruct((tb, nh * CH),...  3.86 us
    unnamed x1, local copies, waits for them, and re-layouts  2.33 us

profile of v2, /device:TPU:1, one launch (start us, length us, event | category | flops | bytes accessed | tf_op | source)
XLA Modules:
  0.0 80.5 jit_solution(5825917507606033975)
XLA Ops:
  0.0 2.3 %copy.12 = bf16[1024,2,256]{2,0,1:T(8,128)(2,1)} copy(bf16[1024,2,256]{2,1,0:T(2,128)(2,1)} %param.11) | data formatting | bytes 2097152 | tf_op args[2]
  2.3 74.3 %shard_map.91 = (bf16[8,8,128,256]{3,2,1,0:T(8,128)(2,1)}, f32[8,1,128]{2,1,0:T(1,128)}) custom-call(bf16[1024,2048]{1,0:T(8,128)(2,1)} %feat_hbm.1, bf16[1024,2048]{1,0:T(8,128)(2,1)} %gate_hbm.1, bf16[2,1024,256]{2,1,0:T(8,128)(2,1)} %bitcast.5, f32[32,1024]{1,0:T(8,128)} %step_hbm.1, f32[32,1024]{1,0:T(8,128)} %decay_hbm.1, bf16[4,2048]{1,0:T(4,128)(2,1)} %cf_hbm.1, ...), custom_call_target="tpu_custom_call" | custom-call | flops 6000000000 | bytes 16000000 | tf_op jit(solution)/shard_map/pallas_call | solution.py:536
  76.7 3.9 %shard_map.92 = bf16[128,16384]{1,0:T(8,128)(2,1)} custom-call(bf16[8,8,128,256]{3,2,1,0:T(8,128)(2,1)} %get-tuple-element.7.z_hbm, f32[8,1,128]{2,1,0:T(1,128)} %get-tuple-element.8.rs_hbm), custom_call_target="tpu_custom_call" | custom-call | flops 4000000 | bytes 8400000 | tf_op jit(solution)/shard_map/pallas_call | solution.py:641

commit v3 on v2

--- a/solution.py
+++ b/solution.py
@@ -134,10 +134,7 @@
     def peer(k):
         return lax.rem(mh + k, nh)
 
-    def sio_in(i):
-        return pltpu.make_async_copy(
-            sio_hbm.at[i], sio.at[i, pl.ds(PAD, TOK)], sio_sem.at[i]
-        )
+    sio_in = pltpu.make_async_copy(sio_hbm, sio.at[pl.ds(PAD, TOK)], sio_sem)
 
     def feat_in(g):
         cols = pl.ds(pl.multiple_of(g * GW, GW), GW)
@@ -164,8 +161,7 @@
     ]
     for copy in small:
         copy.start()
-    for i in range(2):
-        sio_in(i).start()
+    sio_in.start()
 
     @pl.loop(0, NG)
     def _(g):
@@ -173,11 +169,11 @@
 
     bar = pltpu.get_barrier_semaphore()
 
-    @pl.loop(1, nc)
+    @pl.loop(1, nc, unroll=5)
     def _(k):
         pl.semaphore_signal(bar, inc=1, device_id={"ctx": rank(k)}, device_id_type=MESH)
 
-    @pl.loop(1, nh)
+    @pl.loop(1, nh, unroll=7)
     def _(k):
         pl.semaphore_signal(bar, inc=1, device_id={"head": peer(k)}, device_id_type=MESH)
 
@@ -195,15 +191,14 @@
             device_id_type=MESH,
         )
 
-    def halo_map(i):
-        return pltpu.make_async_remote_copy(
-            src_ref=sio_hbm.at[i, pl.ds(TOK - PAD, PAD)],
-            dst_ref=sio.at[i, pl.ds(0, PAD)],
-            send_sem=halo_send.at[NG + i],
-            recv_sem=halo_recv.at[NG + i],
-            device_id={"ctx": nxt},
-            device_id_type=MESH,
-        )
+    halo_map = pltpu.make_async_remote_copy(
+        src_ref=sio_hbm.at[pl.ds(TOK - PAD, PAD)],
+        dst_ref=sio.at[pl.ds(0, PAD)],
+        send_sem=halo_send.at[NG],
+        recv_sem=halo_recv.at[NG],
+        device_id={"ctx": nxt},
+        device_id_type=MESH,
+    )
 
     def four(v):
         return jnp.concatenate([v, v, v, v], axis=0)
@@ -254,16 +249,11 @@
     skip_row[...] = widened(jnp.broadcast_to(skip_ref[...], (8, HEADS)))[0:1]
 
     pl.semaphore_wait(bar, nc - 1 + nh - 1)
-    for i in range(2):
-        halo_map(i).start()
+    halo_map.start()
 
     @pl.loop(0, NG)
     def _(g):
         halo_copy(g).start()
-
-    @pl.loop(0, NG)
-    def _(g):
-        gate_in(g).start()
 
     def d_copy(k):
         return pltpu.make_async_remote_copy(
@@ -278,7 +268,7 @@
     d_own = pltpu.make_async_copy(dsend.at[0], dall.at[me], d_recv_sem)
     d_own.start()
 
-    @pl.loop(1, nc)
+    @pl.loop(1, nc, unroll=5)
     def _(k):
         d_copy(k).start()
 
@@ -293,22 +283,10 @@
             total = total + taps[k : k + 1] * dot(shift[k], block)
         return silu(total)
 
-    def maps(i, store):
-        sio_in(i).wait()
+    def maps(i, store, blocks):
         taps = cs_ref[...].astype(F32)[:, i]
-
-        def one(b):
-            store(b, conv(sio[i, b * BLK : b * BLK + BLK + PAD, :], taps))
-
-        for b in range(1, NB):
-            one(b)
-        halo_map(i).wait()
-
-        @pl.when(me == 0)
-        def _():
-            sio[i, 0:PAD, :] = jnp.zeros((PAD, ST), BF16)
-
-        one(0)
+        for b in blocks:
+            store(b, conv(sio[b * BLK : b * BLK + BLK + PAD, i, :], taps))
 
     def store_in(b, v):
         low = v.astype(BF16)
@@ -319,7 +297,15 @@
     def store_out(b, v):
         out_rows[b * BLK : (b + 1) * BLK, :] = v.astype(BF16)
 
-    maps(0, store_in)
+    sio_in.wait()
+    maps(0, store_in, range(1, NB))
+    halo_map.wait()
+
+    @pl.when(me == 0)
+    def _():
+        sio[0:PAD] = jnp.zeros((PAD, 2, ST), BF16)
+
+    maps(0, store_in, range(1))
 
     def s_copy(g, k):
         return pltpu.make_async_remote_copy(
@@ -376,12 +362,12 @@
         sbuf[g] = state.astype(BF16).reshape(nc, sl, GW)
         pltpu.make_async_copy(sbuf.at[g, me], gath.at[g, me], s_recv.at[g]).start()
 
-        @pl.loop(1, nc)
+        @pl.loop(1, nc, unroll=5)
         def _(k):
             s_copy(g, k).start()
 
     def prepare_b():
-        maps(1, store_out)
+        maps(1, store_out, range(NB))
         inside = r // L == c // L
         mid = L // 2 - 1
         plus = inside & (c % L > mid) & (c <= r)
@@ -414,7 +400,7 @@
             running = dall[q, :, cols] * running + gath[g, q].astype(F32)
         pltpu.make_async_copy(pbuf.at[g, me], inc.at[g, me], p_recv.at[g]).start()
 
-        @pl.loop(1, nc)
+        @pl.loop(1, nc, unroll=5)
         def _(k):
             p_copy(g, k).start()
 
@@ -466,23 +452,29 @@
 
         pltpu.make_async_copy(zsend.at[g, mh], z_out.at[g, mh], z_recv.at[g]).start()
 
-        @pl.loop(1, nh)
+        @pl.loop(1, nh, unroll=7)
         def _(k):
             z_copy(g, k).start()
 
+    def states_by(i):
+        return jnp.clip(jnp.maximum(i + 1, 2 * i - 1), 0, NG)
+
+    def prefixes_by(i):
+        return jnp.clip(jnp.maximum(i, 2 * i - 3), 0, NG)
+
     @pl.loop(0, NG + 2)
     def _(i):
-        @pl.when(i < NG)
-        def _():
-            phase_a(i)
+        pl.loop(states_by(i - 1), states_by(i))(phase_a)
 
         @pl.when(i == 1)
         def _():
+            @pl.loop(0, NG)
+            def _(g):
+                gate_in(g).start()
+
             prepare_b()
 
-        @pl.when((i >= 1) & (i < NG + 1))
-        def _():
-            phase_x(i - 1)
+        pl.loop(prefixes_by(i - 1), prefixes_by(i))(phase_x)
 
         @pl.when(i >= 2)
         def _():
@@ -504,7 +496,7 @@
             device_id_type=MESH,
         )
 
-    @pl.loop(1, nh)
+    @pl.loop(1, nh, unroll=7)
     def _(k):
         r_copy(k).start()
 
@@ -551,7 +543,7 @@
             pltpu.VMEM((1, CH), F32),
             pltpu.VMEM((NG, TOK + PAD, GW), BF16),
             pltpu.VMEM((NG, TOK, GW), BF16),
-            pltpu.VMEM((2, TOK + PAD, ST), BF16),
+            pltpu.VMEM((TOK + PAD, 2, ST), BF16),
             pltpu.VMEM((NG, TOK, GW), BF16),
             pltpu.VMEM((TOK, GW), BF16),
             pltpu.VMEM((TOK, ST), BF16),
@@ -576,9 +568,9 @@
             dma((6,)),
             dma((NG,)),
             dma((NG,)),
-            dma((2,)),
-            dma((NG + 2,)),
-            dma((NG + 2,)),
+            dma,
+            dma((NG + 1,)),
+            dma((NG + 1,)),
             dma,
             dma,
             dma((NG,)),
@@ -662,13 +654,12 @@
     features, gates, state_io, step_size, log_decay, conv_feat, conv_state, skip_gain, norm_gain
 ):
     nc, nh = lax.axis_size("ctx"), lax.axis_size("head")
-    sio = jnp.transpose(state_io, (1, 0, 2))
     z, rs = mixer(
         nc,
         nh,
         features,
         gates,
-        sio,
+        state_io,
         step_size,
         log_decay,
         conv_feat,

time: 80.7 us -> 78.6 us (0.974)
  local copies, waits for them, and re-layouts: 2.33 us -> 0 us
    unnamed x1 -> x0, local copies, waits for them, and re-layouts: 2.33 us -> none
where the time goes in v3:
time: 78.6 us; the launch traced here: 78.5 us
  Pallas kernels  78.5 us (100%)
    pallas_call x1, Pallas kernels, mixer(): pl.pallas_call(functools.partial(mixer_kernel, nc, nh), out_shape=[jax.Sh...  74.6 us
    pallas_call x1, Pallas kernels, normalize(): pl.pallas_call(norm_kernel, out_shape=jax.ShapeDtypeStruct((tb, nh * CH),...  3.86 us

profile of v3, /device:TPU:1, one launch (start us, length us, event | category | flops | bytes accessed | tf_op | source)
XLA Modules:
  0.0 78.5 jit_solution(14055145095693132290)
XLA Ops:
  0.0 74.6 %shard_map.91 = (bf16[8,8,128,256]{3,2,1,0:T(8,128)(2,1)}, f32[8,1,128]{2,1,0:T(1,128)}) custom-call(bf16[1024,2048]{1,0:T(8,128)(2,1)} %feat_hbm.1, bf16[1024,2048]{1,0:T(8,128)(2,1)} %gate_hbm.1, bf16[1024,2,256]{2,1,0:T(2,128)(2,1)} %sio_hbm.1, f32[32,1024]{1,0:T(8,128)} %step_hbm.1, f32[32,1024]{1,0:T(8,128)} %decay_hbm.1, bf16[4,2048]{1,0:T(4,128)(2,1)} %cf_hbm.1, ...), custom_call_target="tpu_custom_call" | custom-call | flops 6000000000 | bytes 16000000 | tf_op jit(solution)/shard_map/pallas_call | solution.py:528
  74.6 3.9 %shard_map.92 = bf16[128,16384]{1,0:T(8,128)(2,1)} custom-call(bf16[8,8,128,256]{3,2,1,0:T(8,128)(2,1)} %get-tuple-element.7.z_hbm, f32[8,1,128]{2,1,0:T(1,128)} %get-tuple-element.8.rs_hbm), custom_call_target="tpu_custom_call" | custom-call | flops 4000000 | bytes 8400000 | tf_op jit(solution)/shard_map/pallas_call | solution.py:633

commit v4 on v3

--- a/solution.py
+++ b/solution.py
@@ -177,8 +177,6 @@
     def _(k):
         pl.semaphore_signal(bar, inc=1, device_id={"head": peer(k)}, device_id_type=MESH)
 
-    for copy in small:
-        copy.wait()
 
     def halo_copy(g):
         cols = pl.ds(pl.multiple_of(g * GW, GW), GW)
@@ -199,6 +197,16 @@
         device_id={"ctx": nxt},
         device_id_type=MESH,
     )
+
+    pl.semaphore_wait(bar, nc - 1 + nh - 1)
+    halo_map.start()
+
+    @pl.loop(0, NG)
+    def _(g):
+        halo_copy(g).start()
+
+    for copy in small:
+        copy.wait()
 
     def four(v):
         return jnp.concatenate([v, v, v, v], axis=0)
@@ -248,13 +256,6 @@
     dsend[0] = widened(jnp.exp(sums[48:56, 0:HEADS]))[0:1]
     skip_row[...] = widened(jnp.broadcast_to(skip_ref[...], (8, HEADS)))[0:1]
 
-    pl.semaphore_wait(bar, nc - 1 + nh - 1)
-    halo_map.start()
-
-    @pl.loop(0, NG)
-    def _(g):
-        halo_copy(g).start()
-
     def d_copy(k):
         return pltpu.make_async_remote_copy(
             src_ref=dsend.at[0],
@@ -327,13 +328,16 @@
             device_id_type=MESH,
         )
 
-    def z_copy(g, k):
+    def z_own(g):
+        return pltpu.make_async_copy(zsend.at[g, mh], z_out.at[g, mh], z_recv.at[g])
+
+    def z_copy(g, to):
         return pltpu.make_async_remote_copy(
-            src_ref=zsend.at[g, peer(k)],
+            src_ref=zsend.at[g, to],
             dst_ref=z_out.at[g, mh],
             send_sem=z_send.at[g],
             recv_sem=z_recv.at[g],
-            device_id={"head": peer(k)},
+            device_id={"head": to},
             device_id_type=MESH,
         )
 
@@ -405,17 +409,16 @@
             p_copy(g, k).start()
 
     def phase_b(g):
-        gate_in(g).wait()
-        pltpu.make_async_copy(inc.at[g], inc.at[g], p_recv.at[g]).wait()
         spread_a, spread_b = expander(g, 0), expander(g, 1)
         cols = pl.ds(pl.multiple_of(g * GW, GW), GW)
         skip = skip_row[:, cols]
         gain = gain_ref[:, cols]
         rows_g[...] = dot(rows_fac[...], spread_a)
+        gate_in(g).wait()
+        pltpu.make_async_copy(inc.at[g], inc.at[g], p_recv.at[g]).wait()
         carry[...] = inc[g].reshape(ST, GW).astype(F32)
 
-        @pl.loop(0, NB, unroll=2)
-        def _(n):
+        def one(n):
             r0 = pl.multiple_of(n * BLK, BLK)
 
             def factor(i):
@@ -450,11 +453,21 @@
                 gated * gain
             ).astype(BF16)
 
-        pltpu.make_async_copy(zsend.at[g, mh], z_out.at[g, mh], z_recv.at[g]).start()
-
-        @pl.loop(1, nh, unroll=7)
-        def _(k):
-            z_copy(g, k).start()
+        half = nh // 2
+        for part in range(2):
+            pl.loop(part * NB // 2, (part + 1) * NB // 2, unroll=4)(one)
+
+            @pl.loop(0, half, unroll=half)
+            def _(k):
+                to = part * half + lax.rem(mh + 1 + k, half)
+
+                @pl.when(to == mh)
+                def _():
+                    z_own(g).start()
+
+                @pl.when(to != mh)
+                def _():
+                    z_copy(g, to).start()
 
     def states_by(i):
         return jnp.clip(jnp.maximum(i + 1, 2 * i - 1), 0, NG)

time: 78.6 us -> 76.7 us (0.976)
  Pallas kernels: 78.5 us -> 76.6 us
    pallas_call x1, Pallas kernels: 74.6 us -> 72.7 us  [mixer(): pl.pallas_call(functools.partial(mixer_kernel, nc, nh), out_shape=[jax.Sh...]
where the time goes in v4:
time: 76.7 us; the launch traced here: 76.6 us
  Pallas kernels  76.6 us (100%)
    pallas_call x1, Pallas kernels, mixer(): pl.pallas_call(functools.partial(mixer_kernel, nc, nh), out_shape=[jax.Sh...  72.7 us
    pallas_call x1, Pallas kernels, normalize(): pl.pallas_call(norm_kernel, out_shape=jax.ShapeDtypeStruct((tb, nh * CH),...  3.86 us

profile of v4, /device:TPU:1, one launch (start us, length us, event | category | flops | bytes accessed | tf_op | source)
XLA Modules:
  0.0 76.6 jit_solution(2247373641539501858)
XLA Ops:
  0.0 72.7 %shard_map.91 = (bf16[8,8,128,256]{3,2,1,0:T(8,128)(2,1)}, f32[8,1,128]{2,1,0:T(1,128)}) custom-call(bf16[1024,2048]{1,0:T(8,128)(2,1)} %feat_hbm.1, bf16[1024,2048]{1,0:T(8,128)(2,1)} %gate_hbm.1, bf16[1024,2,256]{2,1,0:T(2,128)(2,1)} %sio_hbm.1, f32[32,1024]{1,0:T(8,128)} %step_hbm.1, f32[32,1024]{1,0:T(8,128)} %decay_hbm.1, bf16[4,2048]{1,0:T(4,128)(2,1)} %cf_hbm.1, ...), custom_call_target="tpu_custom_call" | custom-call | flops 6000000000 | bytes 16000000 | tf_op jit(solution)/shard_map/pallas_call | solution.py:541
  72.7 3.9 %shard_map.92 = bf16[128,16384]{1,0:T(8,128)(2,1)} custom-call(bf16[8,8,128,256]{3,2,1,0:T(8,128)(2,1)} %get-tuple-element.7.z_hbm, f32[8,1,128]{2,1,0:T(1,128)} %get-tuple-element.8.rs_hbm), custom_call_target="tpu_custom_call" | custom-call | flops 4000000 | bytes 8400000 | tf_op jit(solution)/shard_map/pallas_call | solution.py:646

commit v5 on v4

--- a/solution.py
+++ b/solution.py
@@ -453,9 +453,9 @@
                 gated * gain
             ).astype(BF16)
 
-        half = nh // 2
-        for part in range(2):
-            pl.loop(part * NB // 2, (part + 1) * NB // 2, unroll=4)(one)
+        half = nh // 4
+        for part in range(4):
+            pl.loop(part * NB // 4, (part + 1) * NB // 4, unroll=2)(one)
 
             @pl.loop(0, half, unroll=half)
             def _(k):

time: 76.7 us -> 76.6 us (level)
  no operation moved by 1% of the time
where the time goes in v5:
time: 76.6 us; the launch traced here: 76.4 us
  Pallas kernels  76.4 us (100%)
    pallas_call x1, Pallas kernels, mixer(): pl.pallas_call(functools.partial(mixer_kernel, nc, nh), out_shape=[jax.Sh...  72.6 us
    pallas_call x1, Pallas kernels, normalize(): pl.pallas_call(norm_kernel, out_shape=jax.ShapeDtypeStruct((tb, nh * CH),...  3.86 us

profile of v5, /device:TPU:1, one launch (start us, length us, event | category | flops | bytes accessed | tf_op | source)
XLA Modules:
  0.0 76.4 jit_solution(17815497821555647758)
XLA Ops:
  0.0 72.6 %shard_map.91 = (bf16[8,8,128,256]{3,2,1,0:T(8,128)(2,1)}, f32[8,1,128]{2,1,0:T(1,128)}) custom-call(bf16[1024,2048]{1,0:T(8,128)(2,1)} %feat_hbm.1, bf16[1024,2048]{1,0:T(8,128)(2,1)} %gate_hbm.1, bf16[1024,2,256]{2,1,0:T(2,128)(2,1)} %sio_hbm.1, f32[32,1024]{1,0:T(8,128)} %step_hbm.1, f32[32,1024]{1,0:T(8,128)} %decay_hbm.1, bf16[4,2048]{1,0:T(4,128)(2,1)} %cf_hbm.1, ...), custom_call_target="tpu_custom_call" | custom-call | flops 6000000000 | bytes 16000000 | tf_op jit(solution)/shard_map/pallas_call | solution.py:541
  72.6 3.9 %shard_map.92 = bf16[128,16384]{1,0:T(8,128)(2,1)} custom-call(bf16[8,8,128,256]{3,2,1,0:T(8,128)(2,1)} %get-tuple-element.7.z_hbm, f32[8,1,128]{2,1,0:T(1,128)} %get-tuple-element.8.rs_hbm), custom_call_target="tpu_custom_call" | custom-call | flops 4000000 | bytes 8400000 | tf_op jit(solution)/shard_map/pallas_call | solution.py:646
